TPU v7x, 512 devices: a whole 4x4x16 slice. The times are simulated.
512 devices in a mesh: node: 32 (over y, x, core), head: 16 (over z).
Axes of the slice: x: 4, y: 4, z: 16, core: 2. Of those that a mesh axis runs over, the one named last changes fastest.
Arguments:
- feats: bfloat16 [65536, 512], P('node'), may hold values from -13 to 13
- cot: bfloat16 [65536, 512], P(('node', 'head')), may hold values from -6 to 6
- wq: bfloat16 [512, 512], P(None, 'head'), may hold values from -0.25 to 0.25
- wk: bfloat16 [512, 512], P(None, 'head'), may hold values from -0.25 to 0.25
- wv: bfloat16 [512, 512], P(None, 'head'), may hold values from -0.25 to 0.25
- adj: int32 [512, 4], P('node'), may hold values from 0 to 15
- adj_count: int32 [512], P('node'), may hold values from 1 to 4
- perms: int32 [3, 32, 16], P(None, 'node'), may hold values from 0 to 15, each once within a row
Outputs:
- attn: bfloat16 [65536, 512], P(('node', 'head'))
- grad_x: bfloat16 [65536, 512], P(('node', 'head'))
- grad_wq: float32 [512, 512], P(None, 'head')
- grad_wk: float32 [512, 512], P(None, 'head')
- grad_wv: float32 [512, 512], P(None, 'head')
Inputs may be any that keep to these rules, and one draw needn't show every extreme that they name: Only the first adj_count[b] entries of row b of adj are used; entries index blocks within the group of block b. Each row perms[m, n] holds every number below 16 once.
All inputs are finite; a program needn't handle non-finite values.
Results may differ from a plain program's by a relative error of at most 0.025.
The roundings to bfloat16 on the way count: a program that leaves them out, or rounds other values in their place, can miss the bound.
Values may be sent and summed in bfloat16 or wider, within the bound.
A program may use at most 64 MiB of HBM per device.

v0:
```python
import math

import jax
import jax.numpy as jnp
from jax import lax
from jax.sharding import PartitionSpec as P

HEADS = 8
BLOCK = 128
MAXADJ = 4
MATCH = 3


def slot_table(adj, perms, group):
    own = jnp.arange(group, dtype=jnp.int32)[:, None]
    partner = jnp.transpose(perms[:, 0, :])
    return jnp.concatenate([own, adj, partner], axis=1)


def heads_first(rows_by_width, head_dim):
    return jnp.transpose(rows_by_width.reshape(rows_by_width.shape[0], HEADS, head_dim), (1, 2, 0))


def block_pass(queries, keys, values, allowed, upstream):
    width = queries.shape[1]
    head_dim = width // HEADS
    scale = 1.0 / math.sqrt(head_dim)
    q_t = heads_first(queries, head_dim)
    k_t = heads_first(keys, head_dim)
    v_t = heads_first(values, head_dim)
    g_t = heads_first(upstream, head_dim)
    scores = jnp.einsum("hdq,hdk->hqk", q_t, k_t, preferred_element_type=jnp.float32) * scale
    scores = jnp.where(allowed[None, None, :], scores, -1e30)
    top = jnp.max(scores, axis=-1, keepdims=True)
    expo = jnp.exp(scores - top)
    prob = expo / jnp.sum(expo, axis=-1, keepdims=True)
    prob_low = prob.astype(jnp.bfloat16)
    output = jnp.einsum("hqk,hdk->hdq", prob_low, v_t, preferred_element_type=jnp.float32)
    d_values = jnp.einsum("hqk,hdq->hdk", prob_low, g_t, preferred_element_type=jnp.float32)
    d_prob = jnp.einsum("hdq,hdk->hqk", g_t, v_t, preferred_element_type=jnp.float32)
    centre = jnp.sum(prob * d_prob, axis=-1, keepdims=True)
    d_score = (prob * (d_prob - centre)).astype(jnp.bfloat16)
    d_query = jnp.einsum("hqk,hdk->hdq", d_score, k_t, preferred_element_type=jnp.float32) * scale
    d_keys = jnp.einsum("hqk,hdq->hdk", d_score, q_t, preferred_element_type=jnp.float32) * scale
    output = jnp.transpose(output, (2, 0, 1)).reshape(BLOCK, width)
    d_query = jnp.transpose(d_query, (2, 0, 1)).reshape(BLOCK, width)
    return (output, d_query, d_keys.reshape(width, -1), d_values.reshape(width, -1))


def contract_rows(left, right):
    return lax.dot_general(
        left, right, (((1,), (1,)), ((), ())), preferred_element_type=jnp.float32
    )


def local(feats, cot, wq, wk, wv, adj, adj_count, perms):
    width = feats.shape[1]
    cols = wq.shape[1]
    group = feats.shape[0] // BLOCK
    ways = lax.axis_size("head")
    per_dev = group // ways
    rows = per_dev * BLOCK
    mine = lax.axis_index("head")
    slots = 1 + MAXADJ + MATCH
    flat_ids = slot_table(adj, perms, group).reshape(-1)
    q_cols = jnp.dot(feats, wq, preferred_element_type=jnp.float32).astype(jnp.bfloat16)
    k_cols = jnp.dot(feats, wk, preferred_element_type=jnp.float32).astype(jnp.bfloat16)
    v_cols = jnp.dot(feats, wv, preferred_element_type=jnp.float32).astype(jnp.bfloat16)
    key_vals = jnp.concatenate([k_cols, v_cols], axis=1).reshape(group, BLOCK, 2 * cols)
    send_kv = jnp.take(key_vals, flat_ids, axis=0).reshape(ways, per_dev * slots, BLOCK, 2 * cols)
    send_q = q_cols.reshape(ways, rows, cols)
    recv_q, recv_kv = (
        lax.all_to_all(send_q, "head", split_axis=0, concat_axis=0, tiled=True),
        lax.all_to_all(send_kv, "head", split_axis=0, concat_axis=0, tiled=True),
    )
    queries = jnp.transpose(recv_q, (1, 0, 2)).reshape(per_dev, BLOCK, width)
    split_kv = recv_kv.reshape(ways, per_dev, slots * BLOCK, 2, cols)
    keys = jnp.transpose(split_kv[:, :, :, 0, :], (1, 2, 0, 3)).reshape(
        per_dev, slots * BLOCK, width
    )
    values = jnp.transpose(split_kv[:, :, :, 1, :], (1, 2, 0, 3)).reshape(
        per_dev, slots * BLOCK, width
    )
    counts = lax.dynamic_slice_in_dim(adj_count, mine * per_dev, per_dev)
    slot_pos = jnp.arange(slots, dtype=jnp.int32)
    listed = (slot_pos >= 1) & (slot_pos <= MAXADJ)
    allowed = jnp.logical_not(listed)[None, :] | (slot_pos[None, :] - 1 < counts[:, None])
    allowed = jnp.repeat(allowed, BLOCK, axis=1)
    upstream = cot.reshape(per_dev, BLOCK, width)
    output, d_query, d_keys, d_values = jax.vmap(block_pass)(
        queries, keys, values, allowed, upstream
    )
    attn = output.reshape(rows, width).astype(jnp.bfloat16)
    stacked = jnp.stack([d_keys, d_values], axis=1).reshape(per_dev, 2, ways, cols, slots, BLOCK)
    send_back = jnp.transpose(stacked, (2, 0, 4, 5, 1, 3)).reshape(
        ways, per_dev * slots, BLOCK, 2 * cols
    )
    send_dq = jnp.transpose(d_query.reshape(rows, ways, cols), (1, 0, 2))
    back_q, back_kv = (
        lax.all_to_all(
            send_dq.astype(jnp.bfloat16), "head", split_axis=0, concat_axis=0, tiled=True
        ).astype(send_dq.dtype),
        lax.all_to_all(
            send_back.astype(jnp.bfloat16), "head", split_axis=0, concat_axis=0, tiled=True
        ).astype(send_back.dtype),
    )
    selector = (flat_ids[None, :] == jnp.arange(group, dtype=jnp.int32)[:, None]).astype(
        jnp.float32
    )
    summed = jnp.dot(
        selector,
        back_kv.reshape(group * slots, BLOCK * 2 * cols),
        precision=lax.Precision.HIGHEST,
        preferred_element_type=jnp.float32,
    )
    summed = summed.reshape(group * BLOCK, 2 * cols)
    grad_q = back_q.reshape(group * BLOCK, cols).astype(jnp.bfloat16)
    grad_k = summed[:, :cols].astype(jnp.bfloat16)
    grad_v = summed[:, cols:].astype(jnp.bfloat16)
    outer = (((0,), (0,)), ((), ()))
    part_wq = lax.dot_general(feats, grad_q, outer, preferred_element_type=jnp.float32)
    part_wk = lax.dot_general(feats, grad_k, outer, preferred_element_type=jnp.float32)
    part_wv = lax.dot_general(feats, grad_v, outer, preferred_element_type=jnp.float32)
    grad_wq, grad_wk, grad_wv = (
        lax.psum(part_wq.astype(jnp.bfloat16), "node").astype(jnp.float32),
        lax.psum(part_wk.astype(jnp.bfloat16), "node").astype(jnp.float32),
        lax.psum(part_wv.astype(jnp.bfloat16), "node").astype(jnp.float32),
    )
    grad_x = lax.psum_scatter(
        (contract_rows(grad_q, wq) + contract_rows(grad_k, wk) + contract_rows(grad_v, wv)).astype(
            jnp.bfloat16
        ),
        "head",
        scatter_dimension=0,
        tiled=True,
    )
    return (attn, grad_x, grad_wq, grad_wk, grad_wv)


def solution(mesh):
    return jax.shard_map(
        local,
        mesh=mesh,
        in_specs=(
            P("node", None),
            P(("node", "head"), None),
            P(None, "head"),
            P(None, "head"),
            P(None, "head"),
            P("node", None),
            P("node"),
            P(None, "node", None),
        ),
        out_specs=(
            P(("node", "head"), None),
            P(("node", "head"), None),
            P(None, "head"),
            P(None, "head"),
            P(None, "head"),
        ),
        check_vma=False,
    )
```

profile of v0, /device:TPU:1, one launch (start us, length us, event | category | flops | bytes accessed | tf_op | source)
XLA Modules:
  0.0 440.9 jit_solution(9624448154605430596)
XLA Ops:
  9.8 1.5 convolution_convert_fusion.3
  12.1 2.2 gather_fusion
  14.3 4.3 copy_select_fusion
  18.5 15.9 %all-to-all-start = ((bf16[16,8,128,64]{2,1,3,0:T(8,128)(2,1)}), bf16[16,8,128,64]{2,1,3,0:T(8,128)(2,1)}, u32[]{:S(2)}, u32[]{:S(2)}) async-start(bf16[16,8,128,64]{2,1,3,0:T(8,128)(2,1)} %copy_select_fusion), calls=%async_computation | async-start | bytes 4194304 | tf_op jit(solution)/shard_map/all_to_all | solution.py:74
  37.3 89.1 %all-to-all-done = bf16[16,8,128,64]{2,1,3,0:T(8,128)(2,1)} async-done(((bf16[16,8,128,64]{2,1,3,0:T(8,128)(2,1)}), bf16[16,8,128,64]{2,1,3,0:T(8,128)(2,1)}, u32[]{:S(2)}, u32[]{:S(2)}) %all-to-all-start) | async-done | bytes 2097184 | tf_op jit(solution)/shard_map/all_to_all | solution.py:74
  126.4 11.1 %all-to-all-start.1 = ((bf16[16,128,32]{1,2,0:T(8,128)(2,1)}), bf16[16,128,32]{1,2,0:T(8,128)(2,1)S(1)}, u32[]{:S(2)}, u32[]{:S(2)}) async-start(bf16[16,128,32]{1,2,0:T(8,128)(2,1)} %bitcast.131), calls=%async_computation.1 | async-start | bytes 262144 | tf_op jit(solution)/shard_map/all_to_all | solution.py:73
  137.6 4.2 reshape.163
  141.8 2.8 fusion.31
  144.5 5.0 %all-to-all-done.1 = bf16[16,128,32]{1,2,0:T(8,128)(2,1)S(1)} async-done(((bf16[16,128,32]{1,2,0:T(8,128)(2,1)}), bf16[16,128,32]{1,2,0:T(8,128)(2,1)S(1)}, u32[]{:S(2)}, u32[]{:S(2)}) %all-to-all-start.1) | async-done | bytes 131104 | tf_op jit(solution)/shard_map/all_to_all | solution.py:73
  149.5 3.5 fusion.32
  153.0 3.5 fusion.1
  157.5 1.3 copy-done.1
  158.8 1.5 fusion.8
  160.3 6.5 %all-to-all-start.2 = ((bf16[16,128,32]{1,2,0:T(8,128)(2,1)}), bf16[16,128,32]{1,2,0:T(8,128)(2,1)S(1)}, u32[]{:S(2)}, u32[]{:S(2)}) async-start(bf16[16,128,32]{1,2,0:T(8,128)(2,1)} %bitcast.37), calls=%async_computation.2 | async-start | bytes 262144 | tf_op jit(solution)/shard_map/all_to_all | solution.py:100
  166.8 2.7 convolution_convert_fusion.4
  172.1 1.5 pad_maximum_fusion
  173.6 5.1 %all-to-all-done.2 = bf16[16,128,32]{1,2,0:T(8,128)(2,1)S(1)} async-done(((bf16[16,128,32]{1,2,0:T(8,128)(2,1)}), bf16[16,128,32]{1,2,0:T(8,128)(2,1)S(1)}, u32[]{:S(2)}, u32[]{:S(2)}) %all-to-all-start.2) | async-done | bytes 131104 | tf_op jit(solution)/shard_map/all_to_all | solution.py:100
  178.7 6.4 %all-to-all-start.3 = ((bf16[16,8,128,64]{2,3,1,0:T(8,128)(2,1)}), bf16[16,8,128,64]{2,3,1,0:T(8,128)(2,1)}, u32[]{:S(2)}, u32[]{:S(2)}) async-start(bf16[16,8,128,64]{2,3,1,0:T(8,128)(2,1)} %bitcast.134), calls=%async_computation.3 | async-start | bytes 4194304 | tf_op jit(solution)/shard_map/all_to_all | solution.py:103
  186.5 90.5 %all-to-all-done.3 = bf16[16,8,128,64]{2,3,1,0:T(8,128)(2,1)} async-done(((bf16[16,8,128,64]{2,3,1,0:T(8,128)(2,1)}), bf16[16,8,128,64]{2,3,1,0:T(8,128)(2,1)}, u32[]{:S(2)}, u32[]{:S(2)}) %all-to-all-start.3) | async-done | bytes 2097184 | tf_op jit(solution)/shard_map/all_to_all | solution.py:103
  277.0 4.8 %copy.44 = bf16[16,8,128,64]{3,2,1,0:T(8,128)(2,1)} copy(bf16[16,8,128,64]{2,3,1,0:T(8,128)(2,1)} %all-to-all-done.3) | data formatting | bytes 4194304 | tf_op jit(solution)/shard_map/all_to_all | solution.py:103
  281.8 6.6 %reshape.170 = bf16[128,8192]{1,0:T(8,128)(2,1)} reshape(bf16[16,8,128,64]{3,2,1,0:T(8,128)(2,1)} %copy.44) | data formatting | bytes 4194304 | tf_op jit(solution)/shard_map/reshape | solution.py:112
  288.4 2.0 convolution_convert_fusion
  292.0 1.3 fusion.12
  293.3 2.7 fusion.16
  296.1 2.6 fusion.19
  298.8 5.5 %add_convert_fusion = bf16[2048,512]{1,0:T(8,128)(2,1)} fusion(f32[2048,512]{1,0:T(8,128)} %fusion.16, f32[2048,512]{1,0:T(8,128)} %fusion.19, bf16[512,32]{0,1:T(8,128)(2,1)S(1)} %copy-done.7, bf16[16,128,32]{1,2,0:T(8,128)(2,1)S(1)} %all-to-all-done.2), kind=kOutput, calls=%fused_computation.8 | convolution fusion | flops 70254592 | bytes 10649600 | tf_op jit(solution)/shard_map/dot_general | solution.py:51
  304.4 1.2 copy-done.4
  305.5 3.1 convolution_convert_fusion.5
  309.4 119.9 %all-reduce.3.cloned.1.call-done = (bf16[512,32]{0,1:T(8,128)(2,1)}, bf16[512,32]{0,1:T(8,128)(2,1)}, bf16[512,32]{0,1:T(8,128)(2,1)}) async-done(((bf16[512,32]{0,1:T(8,128)(2,1)}, bf16[512,32]{0,1:T(8,128)(2,1)}, bf16[512,32]{0,1:T(8,128)(2,1)}), (bf16[512,32]{0,1:T(8,128)(2,1)}, bf16[512,32]{0,1:T(8,128)(2,1)}, bf16[512,32]{0,1:T(8,128)(2,1)})) %all-reduce.3.cloned.1.call-update) | async-done | bytes 98320 | tf_op jit(solution)/shard_map/psum | solution.py:125
  429.3 1.4 convert_element_type.110
  430.7 1.4 convert_element_type.113
  432.1 1.4 convert_element_type.116
  (50 shorter events, 12.7 us)
Async XLA Ops:
  8.0 1.8 copy-start
  8.0 3.3 copy-start.5
  18.5 16.0 %copy-start.8 = (bf16[128,512]{1,0:T(8,128)(2,1)S(1)}, bf16[128,512]{1,0:T(8,128)(2,1)}, u32[]{:S(2)}) copy-start(bf16[128,512]{1,0:T(8,128)(2,1)} %param.9) | copy-start | bytes 393220
  18.5 16.1 %copy-start.7 = (bf16[512,32]{0,1:T(8,128)(2,1)S(1)}, bf16[512,32]{0,1:T(8,128)(2,1)}, u32[]{:S(2)}) copy-start(bf16[512,32]{0,1:T(8,128)(2,1)} %param.10) | copy-start | bytes 98308
  18.5 107.8 %all-to-all-start = ((bf16[16,8,128,64]{2,1,3,0:T(8,128)(2,1)}), bf16[16,8,128,64]{2,1,3,0:T(8,128)(2,1)}, u32[]{:S(2)}, u32[]{:S(2)}) async-start(bf16[16,8,128,64]{2,1,3,0:T(8,128)(2,1)} %copy_select_fusion), calls=%async_computation | async-start | bytes 4194304 | tf_op jit(solution)/shard_map/all_to_all | solution.py:74
  34.5 1.6 copy-start.9
  126.4 23.2 %all-to-all-start.1 = ((bf16[16,128,32]{1,2,0:T(8,128)(2,1)}), bf16[16,128,32]{1,2,0:T(8,128)(2,1)S(1)}, u32[]{:S(2)}, u32[]{:S(2)}) async-start(bf16[16,128,32]{1,2,0:T(8,128)(2,1)} %bitcast.131), calls=%async_computation.1 | async-start | bytes 262144 | tf_op jit(solution)/shard_map/all_to_all | solution.py:73
  153.0 3.7 copy-start.3
  157.5 1.3 copy-start.1
  160.3 18.4 %all-to-all-start.2 = ((bf16[16,128,32]{1,2,0:T(8,128)(2,1)}), bf16[16,128,32]{1,2,0:T(8,128)(2,1)S(1)}, u32[]{:S(2)}, u32[]{:S(2)}) async-start(bf16[16,128,32]{1,2,0:T(8,128)(2,1)} %bitcast.37), calls=%async_computation.2 | async-start | bytes 262144 | tf_op jit(solution)/shard_map/all_to_all | solution.py:100
  169.5 1.6 copy-start.2
  178.7 98.3 %all-to-all-start.3 = ((bf16[16,8,128,64]{2,3,1,0:T(8,128)(2,1)}), bf16[16,8,128,64]{2,3,1,0:T(8,128)(2,1)}, u32[]{:S(2)}, u32[]{:S(2)}) async-start(bf16[16,8,128,64]{2,3,1,0:T(8,128)(2,1)} %bitcast.134), calls=%async_computation.3 | async-start | bytes 4194304 | tf_op jit(solution)/shard_map/all_to_all | solution.py:103
  185.1 244.2 %all-reduce.3.cloned.1.call-start = ((), (), s32[]{:S(2)}) async-start(), calls=%async_computation.6 | async-start | bytes 196608 | tf_op jit(solution)/shard_map/psum | solution.py:125
  293.3 2.7 copy-start.6
  298.7 134.8 %reduce-scatter.2.cloned.1.call-start = ((), (), s32[]{:S(2)}) async-start(), calls=%async_computation.5 | async-start | bytes 2228224 | tf_op jit(solution)/shard_map/reduce_scatter | solution.py:129
  304.3 1.2 copy-start.4
Sparse Core Ops, SparseCore 0:
  298.8 130.4 all-reduce.2
Sparse Core Ops, SparseCore 1:
  304.4 63.9 reduce-scatter.1
where the time goes:
time: 442 us; the launch traced here: 441 us
  waiting for transfers between devices  310 us (70%)
  starting transfers between devices  40.2 us (9%)
  matrix products  34 us (8%)
  local copies, waits for them, and re-layouts  29.3 us (7%)
  between operations  15.7 us (4%)
  other arithmetic  12.1 us (3%)
    psum x1, waiting for transfers between devices, local(): lax.psum(part_wq.astype(jnp.bfloat16), 'node').astype(jnp.float32)  120 us
    all_to_all x1, waiting for transfers between devices, local(): lax.all_to_all(send_back.astype(jnp.bfloat16), 'head', split_axis=0, conc...  90.5 us
    all_to_all x1, waiting for transfers between devices, local(): lax.all_to_all(send_kv, 'head', split_axis=0, concat_axis=0, tiled=True)  89.1 us
    all_to_all x1, starting transfers between devices, local(): lax.all_to_all(send_kv, 'head', split_axis=0, concat_axis=0, tiled=True)  15.9 us
    all_to_all x1, starting transfers between devices, local(): lax.all_to_all(send_q, 'head', split_axis=0, concat_axis=0, tiled=True)  11.1 us
    dot_general x3, matrix products, contract_rows(): lax.dot_general(left, right, (((1,), (1,)), ((), ())), preferred_element_...  10.9 us
  transfers between devices with their start and end apart: 6, of which 5 were waited for; matrix products, arithmetic and copies ran while one was open for 7% of the time, Pallas kernels for 0%

commit v1 on v0

v1 whole, which is shorter than its diff:
```python
import functools

import jax
import jax.numpy as jnp
from jax import lax
from jax.experimental import pallas as pl
from jax.experimental.pallas import tpu as pltpu
from jax.sharding import PartitionSpec as P

HEADS = 8
BLOCK = 128
MAXADJ = 4
MATCH = 3
SLOTS = 1 + MAXADJ + MATCH
HD = 64
CORES = 2
MESH = pl.DeviceIdType.MESH
VMEM_BYTES = 40 * 1024 * 1024
NT = (((1,), (1,)), ((), ()))


def vmem():
    return pl.BlockSpec(memory_space=pltpu.VMEM)


def hbm():
    return pl.BlockSpec(memory_space=pltpu.HBM)


def smem():
    return pl.BlockSpec(memory_space=pltpu.SMEM)


def low_lanes(rows):
    return lax.broadcasted_iota(jnp.int32, (rows, 128), 1) < HD


def plan_kernel(group, adj_ref, perms_ref, plan_ref, fill):
    order = group * SLOTS
    last = 2 * group * SLOTS
    for c in range(group):
        fill[c] = 0
    for b in range(group):
        for s in range(SLOTS):
            if s == 0:
                c = b
            elif s <= MAXADJ:
                c = adj_ref[s - 1, b]
            else:
                c = perms_ref[s - 1 - MAXADJ, 0, b]
            plan_ref[b * SLOTS + s] = c
            fill[c] = fill[c] + 1
    at = 0
    for c in range(group):
        n = fill[c]
        fill[c] = at
        at = at + n
        plan_ref[last + c] = at - 1
    for b in range(group):
        for s in range(SLOTS):
            c = plan_ref[b * SLOTS + s]
            at = fill[c]
            plan_ref[order + at] = b * SLOTS + s
            fill[c] = at + 1


def loop(first, stop, act):
    def body(d, carry):
        act(d)
        return carry

    lax.fori_loop(first, stop, body, 0)


def layer_kernel(ways, xs, ys, plan_hbm, counts_hbm, wq_hbm, wv_hbm, wk_hbm, cot_hbm, feats_hbm,
                 r1_ref, r2_ref, all_ref, out_ref,
                 plan, counts, cot, feats, shard, wb, packed, landed, kv, kvt, qs, terms, runs, t1, t2, left, gw,
                 near, line, in_sem, w_send, w_recv, c_send, c_recv, a_send, a_recv, p_send, p_recv, h_send, h_recv,
                 z_send, z_recv, n_send, n_recv, y_send, y_recv, g_send, g_recv):
    node = lax.axis_index("node")
    me = lax.axis_index("head")
    half = lax.rem(me, 2)
    head = me // 2
    partner = me + 1 - 2 * half
    cross = xs * CORES
    nodes = ys * cross
    y = node // cross
    near_me = lax.rem(node, cross)
    core = lax.rem(node, CORES)
    cols, width = wq_hbm.shape
    order = ways * SLOTS
    last = 2 * order
    reach = ways // 2
    barrier = pltpu.get_barrier_semaphore()

    def around(d):
        return (node, lax.rem(me + d, ways))

    def across(d):
        return (lax.rem(node + d, nodes), me)

    def remote(src, dst, send_sem, recv_sem, device):
        return pltpu.make_async_remote_copy(
            src_ref=src, dst_ref=dst, send_sem=send_sem, recv_sem=recv_sem, device_id=device, device_id_type=MESH)

    loop(1, ways, lambda d: pl.semaphore_signal(barrier, inc=1, device_id=around(d), device_id_type=MESH))
    loop(1, nodes, lambda d: pl.semaphore_signal(barrier, inc=1, device_id=across(d), device_id_type=MESH))
    inputs = [
        pltpu.make_async_copy(src, dst, in_sem.at[i])
        for i, (src, dst) in enumerate((
            (wq_hbm, shard.at[0]), (wv_hbm, shard.at[1]), (wk_hbm, shard.at[2]), (cot_hbm, cot),
            (plan_hbm, plan), (counts_hbm, counts), (feats_hbm, feats)))
    ]
    for copy in inputs:
        copy.start()
    for copy in inputs[:4]:
        copy.wait()
    wb[0] = jnp.zeros(wb.shape[1:], wb.dtype)
    wb[pl.ds(1, 3), half] = shard[...]
    low = low_lanes(64)
    for p in range(HEADS // 2):
        pair = cot[:, 128 * p:128 * (p + 1)].astype(jnp.float32)
        first, second = pair[:64], pair[64:]
        packed[2 * p] = jnp.where(low, first, pltpu.roll(second, 64, 1)).astype(jnp.bfloat16)
        packed[2 * p + 1] = jnp.where(low, pltpu.roll(first, 64, 1), second).astype(jnp.bfloat16)
    landed[me] = packed[head]
    pl.semaphore_wait(barrier, (ways - 1) + (nodes - 1))

    w_copy = remote(shard, wb.at[pl.ds(1, 3), half], w_send, w_recv, (node, partner))
    w_copy.start()

    def cot_copy(d):
        dest = lax.rem(me + d, ways)
        return remote(packed.at[dest // 2], landed.at[me], c_send.at[d], c_recv.at[d], (node, dest))

    def tile(n):
        x = lax.rem(n // CORES, xs)
        core = lax.rem(n, CORES)
        rows = cols // CORES
        return (n // cross, pl.ds(pl.multiple_of(core * rows, rows), rows), pl.ds(pl.multiple_of(x * 128, 128), 128))

    def shard_copy(d):
        t, rows, lanes = tile(node)
        return remote(shard.at[t, rows, lanes], all_ref.at[me, t, rows, lanes], a_send.at[d], a_recv.at[d], around(d))

    def plane_copy(n, d):
        t, rows, lanes = tile(n)
        piece = all_ref.at[:, t, rows, lanes]
        return remote(piece, piece, p_send.at[d], p_recv.at[d], across(CORES * d))

    def core_copy(c):
        rows = pl.ds(pl.multiple_of(c * (cols // CORES), cols // CORES), cols // CORES)
        piece = all_ref.at[:, :, rows, :]
        return remote(piece, piece, h_send, h_recv, (node + 1 - 2 * core, me))

    def start_cot(k):
        @pl.when(k > 0)
        def _():
            cot_copy(k).start()

        cot_copy(ways - 1 - k).start()

    loop(0, reach, start_cot)
    carries = y < 3

    @pl.when(carries)
    def _():
        t, rows, lanes = tile(node)
        all_ref[me, t, rows, lanes] = shard[t, rows, lanes]
        loop(1, ways, lambda d: shard_copy(d).start())

    for copy in inputs[4:]:
        copy.wait()
    w_copy.wait()
    weights = wb[...].reshape(4 * HD, width)
    per = 4
    for c in range(ways // per):
        rows = feats[c * per * BLOCK:(c + 1) * per * BLOCK, :]
        out = lax.dot_general(rows, weights, NT, preferred_element_type=jnp.float32)
        for j in range(per):
            b = c * per + j
            part = out[j * BLOCK:(j + 1) * BLOCK]
            qs[b] = (part[:, :128].astype(jnp.bfloat16).astype(jnp.float32) * 0.125).astype(jnp.bfloat16)
            kv[b] = part[:, 128:].astype(jnp.bfloat16)
            kvt[b] = jnp.transpose(part[:, 128:]).astype(jnp.bfloat16)

    def block(b):
        ids = [plan[b * SLOTS + s] for s in range(SLOTS)]
        count = counts[b]
        keys = jnp.concatenate([kv[i] for i in ids], axis=0)
        keys_t = jnp.concatenate([kvt[i] for i in ids], axis=1)
        got = landed[b].astype(jnp.float32)
        cot_rows = jnp.concatenate(
            [jnp.where(low, got, 0.0), jnp.where(low, pltpu.roll(got, 64, 1), 0.0)], axis=0).astype(jnp.bfloat16)
        qc = jnp.concatenate([qs[b], cot_rows], axis=0)
        both = lax.dot_general(keys, qc, NT, preferred_element_type=jnp.float32)
        scores = both[:, :BLOCK]
        d_prob = both[:, BLOCK:]
        bias = jnp.concatenate(
            [jnp.full((BLOCK, 1), jnp.where(s <= count, 0.0, -1e30) if 1 <= s <= MAXADJ else 0.0, jnp.float32)
             for s in range(SLOTS)], axis=0)
        scores = scores + bias
        top = jnp.max(scores, axis=0, keepdims=True)
        expo = jnp.exp(scores - top)
        prob = expo * (1.0 / jnp.sum(expo, axis=0, keepdims=True))
        centre = jnp.sum(prob * d_prob, axis=0, keepdims=True)
        d_score = prob * (d_prob - centre)
        mixed = jnp.concatenate([d_score.astype(jnp.bfloat16), prob.astype(jnp.bfloat16)], axis=1)
        rows = jnp.dot(keys_t, mixed, preferred_element_type=jnp.float32)
        d_query = rows[HD:, :BLOCK] * 0.125
        both_t = jnp.concatenate([rows[:HD, BLOCK:], d_query], axis=0)
        t1[b] = jnp.transpose(both_t).astype(jnp.bfloat16)
        left[b, 0:HD] = d_query.astype(jnp.bfloat16)
        terms[b] = jnp.dot(mixed, qc, preferred_element_type=jnp.float32).reshape(SLOTS, BLOCK, 128)

    def served(d):
        return lax.rem(me + half * d + (1 - half) * (ways - d), ways)

    def z_copy(d, src, dst, k):
        dest = served(d)
        return remote(src.at[dest], dst.at[head], z_send.at[k, d], z_recv.at[k, head], (node, dest))

    def step(k):
        @pl.when(k > 0)
        def _():
            source = lax.rem(me + ways - k, ways)
            remote(packed.at[0], landed.at[source], c_send.at[k], c_recv.at[k], around(k)).wait_recv()

        d = ways - 1 - k
        remote(packed.at[0], landed.at[lax.rem(me + k + 1, ways)], c_send.at[d], c_recv.at[d], around(d)).wait_recv()
        block(lax.rem(me + ways - k, ways))
        block(lax.rem(me + k + 1, ways))
        d = k + half

        @pl.when(jnp.logical_and(d >= 1, d < reach))
        def _():
            z_copy(d, t1, r1_ref, 0).start()

        @pl.when(jnp.logical_and(k == 3, carries))
        def _():
            def landed_piece(d):
                t, rows, lanes = tile(node)
                source = lax.rem(me + ways - d, ways)
                remote(shard.at[t, rows, lanes], all_ref.at[source, t, rows, lanes], a_send.at[d], a_recv.at[d],
                       around(d)).wait()

            loop(1, ways, landed_piece)
            loop(1, nodes // CORES, lambda d: plane_copy(node, d).start())

    loop(0, reach, step)

    def add(r, carry):
        run, before = carry
        entry = plan[order + r]
        here = plan[entry]
        keep = jnp.where(here == before, 1.0, 0.0)
        run = run * keep + terms[entry // SLOTS, lax.rem(entry, SLOTS)]
        runs[r] = run
        return run, here

    lax.fori_loop(0, ways * SLOTS, add, (jnp.zeros((BLOCK, 128), jnp.float32), jnp.int32(-1)), unroll=4)

    def total_of(c):
        total = runs[plan[last + c]]
        t2[c] = total.astype(jnp.bfloat16)
        left[c, HD:3 * HD] = jnp.transpose(total).astype(jnp.bfloat16)

    def total_and_send(j):
        d = reach - 1 - j
        total_of(served(d))
        z_copy(d, t2, r2_ref, 1).start()

    loop(0, reach - 1, total_and_send)
    total_of(me)
    loop(reach, ways, lambda d: total_of(served(d)))
    r1_ref[head] = t1[me]
    r2_ref[head] = t2[me]
    half_cols = HD // 2
    start = pl.multiple_of(half * half_cols, half_cols)
    for t in range(3):
        grads = jnp.concatenate([left[b, pl.ds(t * HD + start, half_cols), :] for b in range(ways)], axis=1)
        gw[t * half_cols:(t + 1) * half_cols, :] = jnp.dot(grads, feats[...], preferred_element_type=jnp.float32)

    def near_node(d):
        return (y * cross + lax.rem(near_me + d, cross), me)

    def y_node(d):
        return (lax.rem(y + d, ys) * cross + near_me, me)

    def piece(index):
        rows = 3 * cols // CORES
        return (pl.ds(pl.multiple_of(lax.rem(index, CORES) * rows, rows), rows),
                pl.ds(pl.multiple_of(index // CORES * 128, 128), 128))

    def near_copy(d):
        rows, lanes = piece(lax.rem(near_me + d, cross))
        return remote(gw.at[rows, lanes], near.at[d], n_send.at[d], n_recv.at[d], near_node(d))

    def y_copy(d):
        return remote(near.at[0], line.at[d], y_send.at[d], y_recv.at[d], y_node(d))

    my_rows, my_lanes = piece(near_me)

    def back_copy(d):
        return remote(line.at[0], out_ref.at[my_rows, my_lanes], g_send.at[d], g_recv.at[d], near_node(d))

    loop(1, cross, lambda d: near_copy(d).start())

    def end_plane(d):
        source = lax.rem(node + nodes - CORES * d, nodes)

        @pl.when(source // cross < 3)
        def _():
            plane_copy(source, d).wait_recv()

    loop(1, nodes // CORES, end_plane)
    core_copy(core).start()
    loop(1, cross, lambda d: near_copy(d).wait())
    total = gw[my_rows, my_lanes]
    for d in range(1, cross):
        total = total + near[d]
    near[0] = total
    loop(1, ys, lambda d: y_copy(d).start())
    loop(1, ys, lambda d: y_copy(d).wait())
    for d in range(1, ys):
        total = total + line[d]
    line[0] = total
    out_ref[my_rows, my_lanes] = total
    loop(1, cross, lambda d: back_copy(d).start())

    def end_back(d):
        back_copy(d).wait_send()
        rows, lanes = piece(lax.rem(near_me + cross - d, cross))
        remote(line.at[0], out_ref.at[rows, lanes], g_send.at[d], g_recv.at[d], near_node(d)).wait_recv()

    loop(1, cross, end_back)
    loop(1, ways, lambda d: cot_copy(d).wait_send())

    @pl.when(carries)
    def _():
        loop(1, nodes // CORES, lambda d: plane_copy(node, d).wait_send())

    core_copy(core).wait_send()
    core_copy(1 - core).wait_recv()

    def end_z(d):
        z_copy(d, t1, r1_ref, 0).wait_send()
        z_copy(d, t2, r2_ref, 1).wait_send()
        other = lax.rem(head + d, reach)
        remote(t1.at[0], r1_ref.at[other], z_send.at[0, d], z_recv.at[0, other], around(d)).wait_recv()
        remote(t2.at[0], r2_ref.at[other], z_send.at[1, d], z_recv.at[1, other], around(d)).wait_recv()

    loop(1, reach, end_z)


def finish_kernel(r1_ref, r2_ref, w_ref, gw_ref, attn_ref, gx_ref, gq_ref, gk_ref, gv_ref):
    low = low_lanes(BLOCK)
    for p in range(HEADS // 2):
        first = r1_ref[2 * p].astype(jnp.float32)
        second = pltpu.roll(r1_ref[2 * p + 1].astype(jnp.float32), 64, 1)
        attn_ref[:, 128 * p:128 * (p + 1)] = jnp.where(low, first, second).astype(jnp.bfloat16)
    total = jnp.zeros(gx_ref.shape, jnp.float32)
    zeros = jnp.zeros((HD, w_ref.shape[-1]), w_ref.dtype)
    for h in range(HEADS):
        wq = jnp.concatenate([zeros, w_ref[2 * h, 0], w_ref[2 * h + 1, 0]], axis=0)
        wvk = jnp.concatenate(
            [w_ref[2 * h, 1], w_ref[2 * h + 1, 1], w_ref[2 * h, 2], w_ref[2 * h + 1, 2]], axis=0)
        total = total + jnp.dot(r1_ref[h], wq, preferred_element_type=jnp.float32)
        total = total + jnp.dot(r2_ref[h], wvk, preferred_element_type=jnp.float32)
    gx_ref[...] = total.astype(jnp.bfloat16)
    cols = HD // 2
    gq_ref[...] = gw_ref[:cols]
    gv_ref[...] = gw_ref[cols:2 * cols]
    gk_ref[...] = gw_ref[2 * cols:]


def params(**kwargs):
    return pltpu.CompilerParams(vmem_limit_bytes=VMEM_BYTES, **kwargs)


def local(xs, ys, feats, cot, wq, wk, wv, adj, adj_count, perms):
    width = feats.shape[1]
    cols = wq.shape[1]
    group = feats.shape[0] // BLOCK
    ways = lax.axis_size("head")
    bf16, f32 = jnp.bfloat16, jnp.float32
    cross = xs * CORES
    nodes = xs * ys * CORES
    dma = pltpu.SemaphoreType.DMA
    sds = jax.ShapeDtypeStruct
    plan = pl.pallas_call(
        functools.partial(plan_kernel, group),
        out_shape=sds((2 * group * SLOTS + group,), jnp.int32),
        in_specs=[smem()] * 2,
        out_specs=smem(),
        scratch_shapes=[pltpu.SMEM((group,), jnp.int32)],
    )(adj.T, perms)
    r1, r2, weights, summed = pl.pallas_call(
        functools.partial(layer_kernel, ways, xs, ys),
        out_shape=(
            sds((HEADS, BLOCK, 128), bf16),
            sds((HEADS, BLOCK, 128), bf16),
            sds((ways, 3, cols, width), bf16),
            sds((3 * cols, width), f32),
        ),
        in_specs=[hbm()] * 7,
        out_specs=(vmem(),) * 4,
        scratch_shapes=[
            pltpu.SMEM((2 * group * SLOTS + group,), jnp.int32),
            pltpu.SMEM((group,), jnp.int32),
            pltpu.VMEM((BLOCK, width), bf16),
            pltpu.VMEM((group * BLOCK, width), bf16),
            pltpu.VMEM((3, cols, width), bf16),
            pltpu.VMEM((4, 2, cols, width), bf16),
            pltpu.VMEM((HEADS, 64, 128), bf16),
            pltpu.VMEM((ways, 64, 128), bf16),
            pltpu.VMEM((group, BLOCK, 128), bf16),
            pltpu.VMEM((group, 128, BLOCK), bf16),
            pltpu.VMEM((group, BLOCK, 128), bf16),
            pltpu.VMEM((group, SLOTS, BLOCK, 128), f32),
            pltpu.VMEM((group * SLOTS, BLOCK, 128), f32),
            pltpu.VMEM((group, BLOCK, 128), bf16),
            pltpu.VMEM((group, BLOCK, 128), bf16),
            pltpu.VMEM((group, 3 * HD, BLOCK), bf16),
            pltpu.VMEM((3 * cols, width), f32),
            pltpu.VMEM((cross, 3 * cols // CORES, 128), f32),
            pltpu.VMEM((ys, 3 * cols // CORES, 128), f32),
            dma((7,)), dma, dma, dma((ways,)), dma((ways,)), dma((ways,)), dma((ways,)),
            dma((nodes // CORES,)), dma((nodes // CORES,)), dma, dma,
            dma((2, ways // 2)), dma((2, ways // 2)), dma((cross,)), dma((cross,)),
            dma((ys,)), dma((ys,)), dma((cross,)), dma((cross,)),
        ],
        compiler_params=params(collective_id=0, has_side_effects=True),
        cost_estimate=pl.CostEstimate(flops=16 * 2 * 1024 * 256 * 384, bytes_accessed=8 << 20, transcendentals=1 << 21),
    )(plan, adj_count, wq.T, wv.T, wk.T, cot, feats)
    attn, grad_x, grad_wq, grad_wk, grad_wv = pl.pallas_call(
        finish_kernel,
        out_shape=(
            sds((BLOCK, width), bf16),
            sds((BLOCK, width), bf16),
            sds((cols, width), f32),
            sds((cols, width), f32),
            sds((cols, width), f32),
        ),
        in_specs=[vmem()] * 4,
        out_specs=(vmem(),) * 5,
        compiler_params=params(),
        cost_estimate=pl.CostEstimate(flops=2 * 128 * 2048 * 512, bytes_accessed=3 << 20, transcendentals=0),
    )(r1, r2, weights, summed)
    return (attn, grad_x, grad_wq.T, grad_wk.T, grad_wv.T)


def solution(mesh):
    nodes = mesh.shape["node"]
    xs = 4 if nodes >= 8 else nodes // CORES
    ys = nodes // (xs * CORES)
    return jax.shard_map(
        functools.partial(local, xs, ys),
        mesh=mesh,
        in_specs=(
            P("node", None),
            P(("node", "head"), None),
            P(None, "head"),
            P(None, "head"),
            P(None, "head"),
            P("node", None),
            P("node"),
            P(None, "node", None),
        ),
        out_specs=(
            P(("node", "head"), None),
            P(("node", "head"), None),
            P(None, "head"),
            P(None, "head"),
            P(None, "head"),
        ),
        check_vma=False,
    )
```

time: 442 us -> 74.6 us (0.17)
  waiting for transfers between devices: 310 us -> 0 us
  Pallas kernels: 0 us -> 67.5 us
  starting transfers between devices: 40.2 us -> 0 us
  matrix products: 34 us -> 0 us
  local copies, waits for them, and re-layouts: 29.3 us -> 6.1 us
  between operations: 15.7 us -> 0.66 us
  other arithmetic: 12.1 us -> 0 us
    all_to_all x4 -> x0, waiting for transfers between devices: 190 us -> none  [the longest x1 90.5 us: local(): lax.all_to_all(send_back.astype(jnp.bfloat16), 'head', split_axis=0, conc...]
    psum x1 -> x0, waiting for transfers between devices: 120 us -> none  [local(): lax.psum(part_wq.astype(jnp.bfloat16), 'node').astype(jnp.float32)]
    pallas_call x0 -> x3, Pallas kernels: none -> 67.5 us  [the longest x1 63.2 us: local(): pl.pallas_call(functools.partial(layer_kernel, ways, xs, ys), out_shape=(...]
    all_to_all x4 -> x0, starting transfers between devices: 39.9 us -> none  [the longest x1 15.9 us: local(): lax.all_to_all(send_kv, 'head', split_axis=0, concat_axis=0, tiled=True)]
    dot_general x15 -> x0, matrix products: 30.5 us -> none  [the longest x3 10.9 us: contract_rows(): lax.dot_general(left, right, (((1,), (1,)), ((), ())), preferred_element_...]
    reshape x5 -> x0, local copies, waits for them, and re-layouts: 11.6 us -> none  [the longest x1 6.6 us: local(): back_kv.reshape(group * slots, BLOCK * 2 * cols)]
    convert_element_type x4 -> x0, other arithmetic: 4.85 us -> none  [the longest x1 1.39 us: local(): lax.psum(part_wk.astype(jnp.bfloat16), 'node').astype(jnp.float32)]
    all_to_all x1 -> x0, local copies, waits for them, and re-layouts: 4.8 us -> none  [local(): lax.all_to_all(send_back.astype(jnp.bfloat16), 'head', split_axis=0, conc...]
  transfers between devices with their start and end apart: 6 -> 0, of which waited for: 5 -> 0; matrix products, arithmetic and copies ran while one was open for 7% -> 0% of each run, Pallas kernels for 0% -> 0%
where the time goes in v1:
time: 74.6 us; the launch traced here: 74.2 us
  Pallas kernels  67.5 us (90%)
  local copies, waits for them, and re-layouts  6.1 us (8%)
    pallas_call x1, Pallas kernels, local(): pl.pallas_call(functools.partial(layer_kernel, ways, xs, ys), out_shape=(...  63.2 us
    unnamed x14, local copies, waits for them, and re-layouts  6.1 us
    pallas_call x1, Pallas kernels, local(): pl.pallas_call(functools.partial(plan_kernel, group), out_shape=sds((2 *...  2.86 us

profile of v1, /device:TPU:1, one launch (start us, length us, event | category | flops | bytes accessed | tf_op | source)
XLA Modules:
  0.0 74.2 jit_solution(17119261582567359670)
XLA Ops:
  0.6 2.9 %shard_map.119.plan_hbm = s32[272]{0:T(512)} custom-call(s32[4,16]{1,0:T(4,128)} %bitcast.10, s32[3,1,16]{2,1,0:T(1,128)} %perms_ref.1), custom_call_target="tpu_custom_call" | custom-call | tf_op jit(solution)/shard_map/pallas_call | solution.py:391
  3.5 0.0 copy-start
  3.5 0.7 copy-done
  4.2 0.0 copy-start.1
  4.2 1.6 %copy-done.1 = bf16[2048,512]{1,0:T(8,128)(2,1)S(1)} copy-done((bf16[2048,512]{1,0:T(8,128)(2,1)S(1)}, bf16[2048,512]{1,0:T(8,128)(2,1)}, u32[]{:S(2)}) %copy-start.1) | copy-done | bytes 2097176
  5.8 0.0 copy-start.2
  5.8 0.9 %copy-done.2 = bf16[128,512]{1,0:T(8,128)(2,1)S(1)} copy-done((bf16[128,512]{1,0:T(8,128)(2,1)S(1)}, bf16[128,512]{1,0:T(8,128)(2,1)}, u32[]{:S(2)}) %copy-start.2) | copy-done | bytes 131096
  6.7 0.0 copy-start.3
  6.7 0.8 %copy-done.3 = bf16[512,32]{0,1:T(8,128)(2,1)S(1)} copy-done((bf16[512,32]{0,1:T(8,128)(2,1)S(1)}, bf16[512,32]{0,1:T(8,128)(2,1)}, u32[]{:S(2)}) %copy-start.3) | copy-done | bytes 32792
  7.4 0.0 copy-start.4
  7.4 0.8 %copy-done.4 = bf16[512,32]{0,1:T(8,128)(2,1)S(1)} copy-done((bf16[512,32]{0,1:T(8,128)(2,1)S(1)}, bf16[512,32]{0,1:T(8,128)(2,1)}, u32[]{:S(2)}) %copy-start.4) | copy-done | bytes 32792
  8.2 0.0 copy-start.5
  8.2 0.8 %copy-done.5 = bf16[512,32]{0,1:T(8,128)(2,1)S(1)} copy-done((bf16[512,32]{0,1:T(8,128)(2,1)S(1)}, bf16[512,32]{0,1:T(8,128)(2,1)}, u32[]{:S(2)}) %copy-start.5) | copy-done | bytes 32792
  9.0 0.0 copy-start.6
  9.0 0.7 copy-done.6
  9.6 63.2 %shard_map.120 = (bf16[8,128,128]{2,1,0:T(8,128)(2,1)S(1)}, bf16[8,128,128]{2,1,0:T(8,128)(2,1)S(1)}, bf16[16,3,32,512]{3,2,1,0:T(8,128)(2,1)S(1)}, f32[96,512]{1,0:T(8,128)S(1)}) custom-call(s32[272]{0:T(512)S(1)} %copy-done, s32[16]{0:T(128)S(1)} %copy-done.6, bf16[32,512]{1,0:T(8,128)(2,1)S(1)} %bitcast.7, bf16[32,512]{1,0:T(8,128)(2,1)S(1)} %bitcast.8, ...), custom_call_target="tpu_custom_call" | custom-call | flops 3221225472 | bytes 8388608 | tf_op jit(solution)/shard_map/pallas_call | solution.py:398
  72.8 1.4 %shard_map.121 = (bf16[128,512]{1,0:T(8,128)(2,1)}, bf16[128,512]{1,0:T(8,128)(2,1)}, f32[32,512]{1,0:T(8,128)}, f32[32,512]{1,0:T(8,128)}, f32[32,512]{1,0:T(8,128)}) custom-call(bf16[8,128,128]{2,1,0:T(8,128)(2,1)S(1)} %get-tuple-element.14.r1_ref, bf16[8,128,128]{2,1,0:T(8,128)(2,1)S(1)} %get-tuple-element.15.r2_ref, ...), custom_call_target="tpu_custom_call" | custom-call | flops 268435456 | bytes 3145728 | tf_op jit(solution)/shard_map/pallas_call | solution.py:436
Async XLA Ops:
  3.5 0.7 copy-start
  4.2 1.6 %copy-start.1 = (bf16[2048,512]{1,0:T(8,128)(2,1)S(1)}, bf16[2048,512]{1,0:T(8,128)(2,1)}, u32[]{:S(2)}) copy-start(bf16[2048,512]{1,0:T(8,128)(2,1)} %feats_hbm.1) | copy-start | bytes 6291460
  5.8 0.9 %copy-start.2 = (bf16[128,512]{1,0:T(8,128)(2,1)S(1)}, bf16[128,512]{1,0:T(8,128)(2,1)}, u32[]{:S(2)}) copy-start(bf16[128,512]{1,0:T(8,128)(2,1)} %cot_hbm.1) | copy-start | bytes 393220
  6.7 0.8 %copy-start.3 = (bf16[512,32]{0,1:T(8,128)(2,1)S(1)}, bf16[512,32]{0,1:T(8,128)(2,1)}, u32[]{:S(2)}) copy-start(bf16[512,32]{0,1:T(8,128)(2,1)} %param.10) | copy-start | bytes 98308
  7.4 0.8 %copy-start.4 = (bf16[512,32]{0,1:T(8,128)(2,1)S(1)}, bf16[512,32]{0,1:T(8,128)(2,1)}, u32[]{:S(2)}) copy-start(bf16[512,32]{0,1:T(8,128)(2,1)} %param.12) | copy-start | bytes 98308
  8.2 0.8 %copy-start.5 = (bf16[512,32]{0,1:T(8,128)(2,1)S(1)}, bf16[512,32]{0,1:T(8,128)(2,1)}, u32[]{:S(2)}) copy-start(bf16[512,32]{0,1:T(8,128)(2,1)} %param.11) | copy-start | bytes 98308
  9.0 0.7 copy-start.6

commit v2 on v1

v2 whole, which is shorter than its diff:
```python
import functools

import jax
import jax.numpy as jnp
from jax import lax
from jax.experimental import pallas as pl
from jax.experimental.pallas import tpu as pltpu
from jax.sharding import PartitionSpec as P

HEADS = 8
BLOCK = 128
MAXADJ = 4
MATCH = 3
SLOTS = 1 + MAXADJ + MATCH
HD = 64
CORES = 2
MESH = pl.DeviceIdType.MESH
VMEM_BYTES = 60 * 1024 * 1024
NT = (((1,), (1,)), ((), ()))


def vmem():
    return pl.BlockSpec(memory_space=pltpu.VMEM)


def hbm():
    return pl.BlockSpec(memory_space=pltpu.HBM)


def smem():
    return pl.BlockSpec(memory_space=pltpu.SMEM)


def low_lanes(rows):
    return lax.broadcasted_iota(jnp.int32, (rows, 128), 1) < HD


def flat(rows, at):
    return pltpu.roll(jnp.concatenate([rows, jnp.zeros((1, 128 - rows.shape[1]), jnp.int32)], axis=1), 16 * at, 1)


def make_plan(adj, perms, plan):
    lane = lax.broadcasted_iota(jnp.int32, (1, 128), 1)
    ids = jnp.where(lane < 16, lane, 0)
    for s in range(MAXADJ):
        ids = ids + flat(adj[s:s + 1, :], 1 + s)
    for m in range(MATCH):
        ids = ids + flat(perms[m], 1 + MAXADJ + m)
    across = lax.broadcasted_iota(jnp.int32, (128, 128), 1)
    down = lax.broadcasted_iota(jnp.int32, (128, 128), 0)

    def column(row):
        return jnp.sum(jnp.where(across == down, jnp.broadcast_to(row, (128, 128)), 0), axis=1, keepdims=True)

    ids_down = column(ids)
    before = ids_down * 128 + down < jnp.broadcast_to(ids * 128 + lane, (128, 128))
    rank = jnp.sum(jnp.where(before, 1, 0), axis=0, keepdims=True)
    order = jnp.sum(jnp.where(column(rank) == across, down, 0), axis=0, keepdims=True)
    last = jnp.sum(jnp.where(ids_down <= across, 1, 0), axis=0, keepdims=True) - 1
    plan[0:1, :] = ids
    plan[1:2, :] = order
    plan[2:3, :] = last
    plan[3:8, :] = jnp.zeros((5, 128), jnp.int32)


def loop(first, stop, act):
    def body(d, carry):
        act(d)
        return carry

    lax.fori_loop(first, stop, body, 0)


def layer_kernel(ways, xs, ys, adj_hbm, perms_hbm, counts_hbm, wq_hbm, wv_hbm, wk_hbm, cot_hbm, feats_hbm,
                 attn_ref, gx_ref, out_ref,
                 plan, counts, adj, perms, plan_rows, cot, feats, shard, wb, packed, landed, kv, kvt, qs, terms, runs, t1, t2, feats_t, gw,
                 near, line, r1_ref, r2_ref, all_ref, in_sem, w_send, w_recv, c_send, c_recv, f_send, f_recv, a_send, a_recv, p_send, p_recv, h_send, h_recv,
                 z_send, z_recv, n_send, n_recv, y_send, y_recv, g_send, g_recv):
    node = lax.axis_index("node")
    me = lax.axis_index("head")
    half = lax.rem(me, 2)
    head = me // 2
    partner = me + 1 - 2 * half
    cross = xs * CORES
    nodes = ys * cross
    y = node // cross
    near_me = lax.rem(node, cross)
    core = lax.rem(node, CORES)
    cols, width = wq_hbm.shape
    reach = ways // 2
    barrier = pltpu.get_barrier_semaphore()

    def around(d):
        return (node, lax.rem(me + d, ways))

    def across(d):
        return (lax.rem(node + d, nodes), me)

    def remote(src, dst, send_sem, recv_sem, device):
        return pltpu.make_async_remote_copy(
            src_ref=src, dst_ref=dst, send_sem=send_sem, recv_sem=recv_sem, device_id=device, device_id_type=MESH)

    loop(1, ways, lambda d: pl.semaphore_signal(barrier, inc=1, device_id=around(d), device_id_type=MESH))
    loop(1, nodes // CORES, lambda d: pl.semaphore_signal(
        barrier, inc=1, device_id=across(CORES * d), device_id_type=MESH))
    for x in range(xs):
        other = y * cross + lax.rem(near_me // CORES + x, xs) * CORES + 1 - core
        pl.semaphore_signal(barrier, inc=1, device_id=(other, me), device_id_type=MESH)
    inputs = [
        pltpu.make_async_copy(src, dst, in_sem.at[i])
        for i, (src, dst) in enumerate((
            (wq_hbm, shard.at[0]), (wv_hbm, shard.at[1]), (wk_hbm, shard.at[2]), (cot_hbm, cot),
            (feats_hbm, feats), (adj_hbm, adj), (perms_hbm, perms), (counts_hbm, counts)))
    ]
    for copy in inputs:
        copy.start()
    for copy in inputs[:4]:
        copy.wait()
    wb[0] = jnp.zeros(wb.shape[1:], wb.dtype)
    wb[pl.ds(1, 3), half] = shard[...]
    low = low_lanes(64)
    for p in range(HEADS // 2):
        pair = cot[:, 128 * p:128 * (p + 1)].astype(jnp.float32)
        first, second = pair[:64], pair[64:]
        packed[2 * p] = jnp.where(low, first, pltpu.roll(second, 64, 1)).astype(jnp.bfloat16)
        packed[2 * p + 1] = jnp.where(low, pltpu.roll(first, 64, 1), second).astype(jnp.bfloat16)
    landed[me] = packed[head]
    pl.semaphore_wait(barrier, (ways - 1) + (nodes // CORES - 1) + xs)

    w_copy = remote(shard, wb.at[pl.ds(1, 3), half], w_send, w_recv, (node, partner))
    w_copy.start()

    def served(d):
        return lax.rem(me + half * d + (1 - half) * (ways - d), ways)

    def passed(d):
        return lax.rem(partner + (1 - half) * d + half * (ways - d), ways)

    def cot_copy(d):
        down = lax.rem(me + d, 2)
        dest = lax.rem(me + (1 - down) * d + down * (ways - d), ways)
        return remote(packed.at[dest // 2], landed.at[me], c_send.at[d], c_recv.at[d], (node, dest))

    def pass_copy(d):
        block = served(d)
        return remote(landed.at[block], landed.at[block], f_send.at[d], f_recv.at[d], (node, partner))

    def tile(n):
        x = lax.rem(n // CORES, xs)
        core = lax.rem(n, CORES)
        rows = cols // CORES
        return (n // cross, pl.ds(pl.multiple_of(core * rows, rows), rows), pl.ds(pl.multiple_of(x * 128, 128), 128))

    def shard_copy(d):
        t, rows, lanes = tile(node)
        return remote(shard.at[t, rows, lanes], all_ref.at[me, t, rows, lanes], a_send.at[d], a_recv.at[d], around(d))

    def plane_copy(n, d):
        t, rows, lanes = tile(n)
        piece = all_ref.at[:, t, rows, lanes]
        return remote(piece, piece, p_send.at[d], p_recv.at[d], across(CORES * d))

    def core_copy(c):
        rows = pl.ds(pl.multiple_of(c * (cols // CORES), cols // CORES), cols // CORES)
        piece = all_ref.at[:, :, rows, :]
        return remote(piece, piece, h_send, h_recv, (node + 1 - 2 * core, me))

    carries = y < 3

    loop(1, reach, lambda d: cot_copy(d).start())
    pass_copy(0).start()

    @pl.when(carries)
    def _():
        t, rows, lanes = tile(node)
        all_ref[me, t, rows, lanes] = shard[t, rows, lanes]
        loop(1, ways, lambda d: shard_copy(d).start())

    for copy in inputs[4:]:
        copy.wait()
    make_plan(adj, perms, plan_rows)
    plan_copy = pltpu.make_async_copy(plan_rows, plan, in_sem.at[8])
    plan_copy.start()
    for b in range(ways):
        feats_t[:, b * BLOCK:(b + 1) * BLOCK] = jnp.transpose(feats[b * BLOCK:(b + 1) * BLOCK, :])
    plan_copy.wait()
    w_copy.wait()
    weights = wb[...].reshape(4 * HD, width)
    per = 4
    for c in range(ways // per):
        rows = feats[c * per * BLOCK:(c + 1) * per * BLOCK, :]
        out = lax.dot_general(rows, weights, NT, preferred_element_type=jnp.float32)
        for j in range(per):
            b = c * per + j
            part = out[j * BLOCK:(j + 1) * BLOCK]
            qs[b] = (part[:, :128].astype(jnp.bfloat16).astype(jnp.float32) * 0.125).astype(jnp.bfloat16)
            kv[b] = part[:, 128:].astype(jnp.bfloat16)
            kvt[b] = jnp.transpose(part[:, 128:]).astype(jnp.bfloat16)

    def block(b):
        ids = [plan[0, s * ways + b] for s in range(SLOTS)]
        count = counts[b]
        keys = jnp.concatenate([kv[i] for i in ids], axis=0)
        keys_t = jnp.concatenate([kvt[i] for i in ids], axis=1)
        got = landed[b].astype(jnp.float32)
        cot_rows = jnp.concatenate(
            [jnp.where(low, got, 0.0), jnp.where(low, pltpu.roll(got, 64, 1), 0.0)], axis=0).astype(jnp.bfloat16)
        qc = jnp.concatenate([qs[b], cot_rows], axis=0)
        both = lax.dot_general(keys, qc, NT, preferred_element_type=jnp.float32)
        scores = both[:, :BLOCK]
        d_prob = both[:, BLOCK:]
        bias = jnp.concatenate(
            [jnp.full((BLOCK, 1), jnp.where(s <= count, 0.0, -1e30) if 1 <= s <= MAXADJ else 0.0, jnp.float32)
             for s in range(SLOTS)], axis=0)
        scores = scores + bias
        top = jnp.max(scores, axis=0, keepdims=True)
        expo = jnp.exp(scores - top)
        prob = expo * (1.0 / jnp.sum(expo, axis=0, keepdims=True))
        centre = jnp.sum(prob * d_prob, axis=0, keepdims=True)
        d_score = prob * (d_prob - centre)
        mixed = jnp.concatenate([d_score.astype(jnp.bfloat16), prob.astype(jnp.bfloat16)], axis=1)
        rows = jnp.dot(keys_t, mixed, preferred_element_type=jnp.float32)
        d_query = rows[HD:, :BLOCK] * 0.125
        both_t = jnp.concatenate([rows[:HD, BLOCK:], d_query], axis=0)
        t1[b] = jnp.transpose(both_t).astype(jnp.bfloat16)
        terms[b] = jnp.dot(mixed, qc, preferred_element_type=jnp.float32).reshape(SLOTS, BLOCK, 128)

    def z_copy(d, src, dst, k):
        dest = served(d)
        return remote(src.at[dest], dst.at[head], z_send.at[k, d], z_recv.at[k, head], (node, dest))

    def arrive(d):
        source = served(d)
        remote(packed.at[0], landed.at[source], c_send.at[d], c_recv.at[d], (node, source)).wait_recv()
        pass_copy(d).start()

    def direct(k):
        @pl.when(k > 0)
        def _():
            arrive(2 * k)

        arrive(2 * k + 1)
        block(served(2 * k))
        block(served(2 * k + 1))

        @pl.when(k > 0)
        def _():
            z_copy(2 * k, t1, r1_ref, 0).start()

        z_copy(2 * k + 1, t1, r1_ref, 0).start()

    def second(k):
        for d in (2 * k, 2 * k + 1):
            other = landed.at[passed(d)]
            remote(other, other, f_send.at[d], f_recv.at[d], (node, partner)).wait_recv()
        block(passed(2 * k))
        block(passed(2 * k + 1))

    loop(0, reach // 2, direct)

    @pl.when(carries)
    def _():
        def landed_piece(d):
            t, rows, lanes = tile(node)
            source = lax.rem(me + ways - d, ways)
            remote(shard.at[t, rows, lanes], all_ref.at[source, t, rows, lanes], a_send.at[d], a_recv.at[d],
                   around(d)).wait()

        loop(1, ways, landed_piece)
        loop(1, nodes // CORES, lambda d: plane_copy(node, d).start())

    loop(0, reach // 2, second)

    def add(r, carry):
        run, before = carry
        entry = plan[1, r]
        here = plan[0, entry]
        keep = jnp.where(here == before, 1.0, 0.0)
        run = run * keep + terms[lax.rem(entry, ways), entry // ways]
        runs[r] = run
        return run, here

    lax.fori_loop(0, ways * SLOTS, add, (jnp.zeros((BLOCK, 128), jnp.float32), jnp.int32(-1)), unroll=8)

    def total_of(c):
        t2[c] = runs[plan[2, c]].astype(jnp.bfloat16)

    def total_and_send(j):
        d = reach - 1 - j
        total_of(served(d))
        z_copy(d, t2, r2_ref, 1).start()

    loop(0, reach - 1, total_and_send)
    total_of(me)
    for d in range(reach, ways):
        total_of(served(d))
    r1_ref[head] = t1[me]
    r2_ref[head] = t2[me]
    rows_all = ways * BLOCK
    grads = jnp.concatenate([t1[...].reshape(rows_all, 128), t2[...].reshape(rows_all, 128)], axis=1)
    outer = jnp.dot(feats_t[...], grads, preferred_element_type=jnp.float32)
    one, two = outer[:, :128], outer[:, 128:]
    lane = lax.broadcasted_iota(jnp.int32, one.shape, 1)
    first_half = half == 0
    q_part = jnp.where(first_half, pltpu.roll(one, 64, 1), pltpu.roll(one, 32, 1))
    v_part = jnp.where(first_half, pltpu.roll(two, 32, 1), two)
    k_part = jnp.where(first_half, two, pltpu.roll(two, 96, 1))
    gw[...] = jnp.transpose(jnp.where(lane < 32, q_part, jnp.where(lane < 64, v_part, k_part)))[:3 * cols]

    def near_node(d):
        return (y * cross + lax.rem(near_me + d, cross), me)

    def y_node(d):
        return (lax.rem(y + d, ys) * cross + near_me, me)

    def piece(index):
        rows = 3 * cols // CORES
        return (pl.ds(pl.multiple_of(lax.rem(index, CORES) * rows, rows), rows),
                pl.ds(pl.multiple_of(index // CORES * 128, 128), 128))

    def near_copy(d):
        rows, lanes = piece(lax.rem(near_me + d, cross))
        return remote(gw.at[rows, lanes], near.at[d], n_send.at[d], n_recv.at[d], near_node(d))

    def y_copy(d):
        return remote(near.at[0], line.at[d], y_send.at[d], y_recv.at[d], y_node(d))

    my_rows, my_lanes = piece(near_me)

    def back_copy(d):
        return remote(line.at[0], out_ref.at[my_rows, my_lanes], g_send.at[d], g_recv.at[d], near_node(d))

    loop(1, cross, lambda d: near_copy(d).start())

    def end_plane(d):
        source = lax.rem(node + nodes - CORES * d, nodes)

        @pl.when(source // cross < 3)
        def _():
            plane_copy(source, d).wait_recv()

    loop(1, nodes // CORES, end_plane)
    core_copy(core).start()
    loop(1, cross, lambda d: near_copy(d).wait())
    total = gw[my_rows, my_lanes]
    for d in range(1, cross):
        total = total + near[d]
    near[0] = total
    loop(1, ys, lambda d: y_copy(d).start())

    def end_first(d):
        z_copy(d, t1, r1_ref, 0).wait_send()
        other = lax.rem(head + d, reach)
        remote(t1.at[0], r1_ref.at[other], z_send.at[0, d], z_recv.at[0, other], around(d)).wait_recv()

    loop(1, reach, end_first)
    low_all = low_lanes(BLOCK)
    for p in range(HEADS // 2):
        first = r1_ref[2 * p].astype(jnp.float32)
        second_head = pltpu.roll(r1_ref[2 * p + 1].astype(jnp.float32), 64, 1)
        attn_ref[:, 128 * p:128 * (p + 1)] = jnp.where(low_all, first, second_head).astype(jnp.bfloat16)
    loop(1, ys, lambda d: y_copy(d).wait())
    for d in range(1, ys):
        total = total + line[d]
    line[0] = total
    out_ref[my_rows, my_lanes] = total
    loop(1, cross, lambda d: back_copy(d).start())

    core_copy(core).wait_send()
    core_copy(1 - core).wait_recv()
    grad = jnp.zeros(gx_ref.shape, jnp.float32)
    zeros = jnp.zeros((HD, width), jnp.bfloat16)
    for h in range(HEADS):
        wq = jnp.concatenate([zeros, all_ref[2 * h, 0], all_ref[2 * h + 1, 0]], axis=0)
        grad = grad + jnp.dot(r1_ref[h], wq, preferred_element_type=jnp.float32)

    def end_last(d):
        z_copy(d, t2, r2_ref, 1).wait_send()
        other = lax.rem(head + d, reach)
        remote(t2.at[0], r2_ref.at[other], z_send.at[1, d], z_recv.at[1, other], around(d)).wait_recv()

    loop(1, reach, end_last)
    for h in range(HEADS):
        wvk = jnp.concatenate(
            [all_ref[2 * h, 1], all_ref[2 * h + 1, 1], all_ref[2 * h, 2], all_ref[2 * h + 1, 2]], axis=0)
        grad = grad + jnp.dot(r2_ref[h], wvk, preferred_element_type=jnp.float32)
    gx_ref[...] = grad.astype(jnp.bfloat16)

    def end_back(d):
        back_copy(d).wait_send()
        rows, lanes = piece(lax.rem(near_me + cross - d, cross))
        remote(line.at[0], out_ref.at[rows, lanes], g_send.at[d], g_recv.at[d], near_node(d)).wait_recv()

    loop(1, cross, end_back)
    loop(1, reach, lambda d: cot_copy(d).wait_send())
    loop(0, reach, lambda d: pass_copy(d).wait_send())

    @pl.when(carries)
    def _():
        loop(1, nodes // CORES, lambda d: plane_copy(node, d).wait_send())


def finish_kernel(attn_in, gx_in, gw_ref, attn_ref, gx_ref, gq_ref, gk_ref, gv_ref):
    cols = HD // 2
    attn_ref[...] = attn_in[...]
    gx_ref[...] = gx_in[...]
    gq_ref[...] = gw_ref[:cols]
    gv_ref[...] = gw_ref[cols:2 * cols]
    gk_ref[...] = gw_ref[2 * cols:]


def params(**kwargs):
    return pltpu.CompilerParams(vmem_limit_bytes=VMEM_BYTES, **kwargs)


def local(xs, ys, feats, cot, wq, wk, wv, adj, adj_count, perms):
    width = feats.shape[1]
    cols = wq.shape[1]
    group = feats.shape[0] // BLOCK
    ways = lax.axis_size("head")
    bf16, f32 = jnp.bfloat16, jnp.float32
    cross = xs * CORES
    nodes = xs * ys * CORES
    dma = pltpu.SemaphoreType.DMA
    sds = jax.ShapeDtypeStruct
    attn, grad_x, summed = pl.pallas_call(
        functools.partial(layer_kernel, ways, xs, ys),
        out_shape=(sds((BLOCK, width), bf16), sds((BLOCK, width), bf16), sds((3 * cols, width), f32)),
        in_specs=[hbm()] * 8,
        out_specs=(vmem(),) * 3,
        scratch_shapes=[
            pltpu.SMEM((8, 128), jnp.int32),
            pltpu.SMEM((group,), jnp.int32),
            pltpu.VMEM((MAXADJ, group), jnp.int32),
            pltpu.VMEM((MATCH, 1, group), jnp.int32),
            pltpu.VMEM((8, 128), jnp.int32),
            pltpu.VMEM((BLOCK, width), bf16),
            pltpu.VMEM((group * BLOCK, width), bf16),
            pltpu.VMEM((3, cols, width), bf16),
            pltpu.VMEM((4, 2, cols, width), bf16),
            pltpu.VMEM((HEADS, 64, 128), bf16),
            pltpu.VMEM((ways, 64, 128), bf16),
            pltpu.VMEM((group, BLOCK, 128), bf16),
            pltpu.VMEM((group, 128, BLOCK), bf16),
            pltpu.VMEM((group, BLOCK, 128), bf16),
            pltpu.VMEM((group, SLOTS, BLOCK, 128), f32),
            pltpu.VMEM((group * SLOTS, BLOCK, 128), f32),
            pltpu.VMEM((group, BLOCK, 128), bf16),
            pltpu.VMEM((group, BLOCK, 128), bf16),
            pltpu.VMEM((width, group * BLOCK), bf16),
            pltpu.VMEM((3 * cols, width), f32),
            pltpu.VMEM((cross, 3 * cols // CORES, 128), f32),
            pltpu.VMEM((ys, 3 * cols // CORES, 128), f32),
            pltpu.VMEM((HEADS, BLOCK, 128), bf16),
            pltpu.VMEM((HEADS, BLOCK, 128), bf16),
            pltpu.VMEM((ways, 3, cols, width), bf16),
            dma((9,)), dma, dma, dma((ways // 2,)), dma((ways // 2,)), dma((ways // 2,)), dma((ways // 2,)), dma((ways,)), dma((ways,)),
            dma((nodes // CORES,)), dma((nodes // CORES,)), dma, dma,
            dma((2, ways // 2)), dma((2, ways // 2)), dma((cross,)), dma((cross,)),
            dma((ys,)), dma((ys,)), dma((cross,)), dma((cross,)),
        ],
        compiler_params=params(collective_id=0, has_side_effects=True),
        cost_estimate=pl.CostEstimate(flops=16 * 2 * 1024 * 256 * 384, bytes_accessed=8 << 20, transcendentals=1 << 21),
    )(adj.T, perms, adj_count, wq.T, wv.T, wk.T, cot, feats)
    attn, grad_x, grad_wq, grad_wk, grad_wv = pl.pallas_call(
        finish_kernel,
        out_shape=(
            sds((BLOCK, width), bf16),
            sds((BLOCK, width), bf16),
            sds((cols, width), f32),
            sds((cols, width), f32),
            sds((cols, width), f32),
        ),
        in_specs=[vmem()] * 3,
        out_specs=(vmem(),) * 5,
        compiler_params=params(),
        cost_estimate=pl.CostEstimate(flops=0, bytes_accessed=1 << 20, transcendentals=0),
    )(attn, grad_x, summed)
    return (attn, grad_x, grad_wq.T, grad_wk.T, grad_wv.T)


def solution(mesh):
    nodes = mesh.shape["node"]
    xs = 4 if nodes >= 8 else nodes // CORES
    ys = nodes // (xs * CORES)
    return jax.shard_map(
        functools.partial(local, xs, ys),
        mesh=mesh,
        in_specs=(
            P("node", None),
            P(("node", "head"), None),
            P(None, "head"),
            P(None, "head"),
            P(None, "head"),
            P("node", None),
            P("node"),
            P(None, "node", None),
        ),
        out_specs=(
            P(("node", "head"), None),
            P(("node", "head"), None),
            P(None, "head"),
            P(None, "head"),
            P(None, "head"),
        ),
        check_vma=False,
    )
```

time: 74.6 us -> 60.5 us (0.81)
  Pallas kernels: 67.5 us -> 59.7 us
  local copies, waits for them, and re-layouts: 6.1 us -> 0 us
    unnamed x14 -> x0, local copies, waits for them, and re-layouts: 6.1 us -> none
    pallas_call x1, Pallas kernels: 63.2 us -> 57.9 us  [local(): pl.pallas_call(functools.partial(layer_kernel, ways, xs, ys), out_shape=(...]
    pallas_call x1 -> x0, Pallas kernels: 2.86 us -> none  [local(): pl.pallas_call(functools.partial(plan_kernel, group), out_shape=sds((2 *...]
where the time goes in v2:
time: 60.5 us; the launch traced here: 60.3 us
  Pallas kernels  59.7 us (99%)
  between operations  0.64 us (1%)
    pallas_call x1, Pallas kernels, local(): pl.pallas_call(functools.partial(layer_kernel, ways, xs, ys), out_shape=(...  57.9 us
    pallas_call x1, Pallas kernels, local(): pl.pallas_call(finish_kernel, out_shape=(sds((BLOCK, width), bf16), sds((...  1.82 us

profile of v2, /device:TPU:1, one launch (start us, length us, event | category | flops | bytes accessed | tf_op | source)
XLA Modules:
  0.0 60.3 jit_solution(1935399707814107260)
XLA Ops:
  0.6 57.9 %shard_map.119 = (bf16[128,512]{1,0:T(8,128)(2,1)}, bf16[128,512]{1,0:T(8,128)(2,1)}, f32[96,512]{1,0:T(8,128)}) custom-call(s32[4,16]{1,0:T(4,128)} %bitcast.13, s32[3,1,16]{2,1,0:T(1,128)} %perms_hbm.1, s32[16]{0:T(128)} %counts_hbm.1, bf16[32,512]{1,0:T(8,128)(2,1)} %bitcast.10, bf16[32,512]{1,0:T(8,128)(2,1)} %bitcast.11, bf16[32,512]{1,0:T(8,128)(2,1)} %bitcast.12, ...), custom_call_target="tpu_custom_call" | custom-call | flops 3221225472 | bytes 8388608 | tf_op jit(solution)/shard_map/pallas_call | solution.py:426
  58.5 1.8 %shard_map.120 = (bf16[128,512]{1,0:T(8,128)(2,1)}, bf16[128,512]{1,0:T(8,128)(2,1)}, f32[32,512]{1,0:T(8,128)}, f32[32,512]{1,0:T(8,128)}, f32[32,512]{1,0:T(8,128)}) custom-call(bf16[128,512]{1,0:T(8,128)(2,1)} %get-tuple-element.13.attn_in, bf16[128,512]{1,0:T(8,128)(2,1)} %get-tuple-element.14.gx_in, f32[96,512]{1,0:T(8,128)} %get-tuple-element.15.gw_ref), custom_call_target="tpu_custom_call" | custom-call | bytes 1048576 | tf_op jit(solution)/shard_map/pallas_call | solution.py:465

commit v3 on v2

--- a/solution.py
+++ b/solution.py
@@ -125,57 +125,6 @@
         packed[2 * p] = jnp.where(low, first, pltpu.roll(second, 64, 1)).astype(jnp.bfloat16)
         packed[2 * p + 1] = jnp.where(low, pltpu.roll(first, 64, 1), second).astype(jnp.bfloat16)
     landed[me] = packed[head]
-    pl.semaphore_wait(barrier, (ways - 1) + (nodes // CORES - 1) + xs)
-
-    w_copy = remote(shard, wb.at[pl.ds(1, 3), half], w_send, w_recv, (node, partner))
-    w_copy.start()
-
-    def served(d):
-        return lax.rem(me + half * d + (1 - half) * (ways - d), ways)
-
-    def passed(d):
-        return lax.rem(partner + (1 - half) * d + half * (ways - d), ways)
-
-    def cot_copy(d):
-        down = lax.rem(me + d, 2)
-        dest = lax.rem(me + (1 - down) * d + down * (ways - d), ways)
-        return remote(packed.at[dest // 2], landed.at[me], c_send.at[d], c_recv.at[d], (node, dest))
-
-    def pass_copy(d):
-        block = served(d)
-        return remote(landed.at[block], landed.at[block], f_send.at[d], f_recv.at[d], (node, partner))
-
-    def tile(n):
-        x = lax.rem(n // CORES, xs)
-        core = lax.rem(n, CORES)
-        rows = cols // CORES
-        return (n // cross, pl.ds(pl.multiple_of(core * rows, rows), rows), pl.ds(pl.multiple_of(x * 128, 128), 128))
-
-    def shard_copy(d):
-        t, rows, lanes = tile(node)
-        return remote(shard.at[t, rows, lanes], all_ref.at[me, t, rows, lanes], a_send.at[d], a_recv.at[d], around(d))
-
-    def plane_copy(n, d):
-        t, rows, lanes = tile(n)
-        piece = all_ref.at[:, t, rows, lanes]
-        return remote(piece, piece, p_send.at[d], p_recv.at[d], across(CORES * d))
-
-    def core_copy(c):
-        rows = pl.ds(pl.multiple_of(c * (cols // CORES), cols // CORES), cols // CORES)
-        piece = all_ref.at[:, :, rows, :]
-        return remote(piece, piece, h_send, h_recv, (node + 1 - 2 * core, me))
-
-    carries = y < 3
-
-    loop(1, reach, lambda d: cot_copy(d).start())
-    pass_copy(0).start()
-
-    @pl.when(carries)
-    def _():
-        t, rows, lanes = tile(node)
-        all_ref[me, t, rows, lanes] = shard[t, rows, lanes]
-        loop(1, ways, lambda d: shard_copy(d).start())
-
     for copy in inputs[4:]:
         copy.wait()
     make_plan(adj, perms, plan_rows)
@@ -183,6 +132,60 @@
     plan_copy.start()
     for b in range(ways):
         feats_t[:, b * BLOCK:(b + 1) * BLOCK] = jnp.transpose(feats[b * BLOCK:(b + 1) * BLOCK, :])
+    pl.semaphore_wait(barrier, (ways - 1) + (nodes // CORES - 1) + xs)
+
+    w_copy = remote(shard, wb.at[pl.ds(1, 3), half], w_send, w_recv, (node, partner))
+    w_copy.start()
+
+    def served(d):
+        return lax.rem(me + half * d + (1 - half) * (ways - d), ways)
+
+    def passed(d):
+        return lax.rem(partner + (1 - half) * d + half * (ways - d), ways)
+
+    def cot_copy(d):
+        down = lax.rem(me + d, 2)
+        dest = lax.rem(me + (1 - down) * d + down * (ways - d), ways)
+        return remote(packed.at[dest // 2], landed.at[me], c_send, c_recv.at[d], (node, dest))
+
+    def pass_copy(d):
+        block = served(d)
+        return remote(landed.at[block], landed.at[block], f_send, f_recv.at[d], (node, partner))
+
+    def tile(n):
+        x = lax.rem(n // CORES, xs)
+        core = lax.rem(n, CORES)
+        rows = cols // CORES
+        return (n // cross, pl.ds(pl.multiple_of(core * rows, rows), rows), pl.ds(pl.multiple_of(x * 128, 128), 128))
+
+    def shard_copy(d):
+        t, rows, lanes = tile(node)
+        return remote(shard.at[t, rows, lanes], all_ref.at[me, t, rows, lanes], a_send, a_recv, around(d))
+
+    def plane_copy(n, d):
+        t, rows, lanes = tile(n)
+        piece = all_ref.at[:, t, rows, lanes]
+        return remote(piece, piece, p_send, p_recv, across(CORES * d))
+
+    def core_copy(c):
+        rows = pl.ds(pl.multiple_of(c * (cols // CORES), cols // CORES), cols // CORES)
+        piece = all_ref.at[:, :, rows, :]
+        return remote(piece, piece, h_send, h_recv, (node + 1 - 2 * core, me))
+
+    carries = y < 3
+
+    def all_bytes(rows, send_sem, recv_sem):
+        return remote(rows, rows, send_sem, recv_sem, (node, partner))
+
+    @pl.when(carries)
+    def _():
+        t, rows, lanes = tile(node)
+        all_ref[me, t, rows, lanes] = shard[t, rows, lanes]
+        loop(1, ways, lambda d: shard_copy(d).start())
+
+    loop(1, reach, lambda d: cot_copy(d).start())
+    pass_copy(0).start()
+
     plan_copy.wait()
     w_copy.wait()
     weights = wb[...].reshape(4 * HD, width)
@@ -207,16 +210,16 @@
             [jnp.where(low, got, 0.0), jnp.where(low, pltpu.roll(got, 64, 1), 0.0)], axis=0).astype(jnp.bfloat16)
         qc = jnp.concatenate([qs[b], cot_rows], axis=0)
         both = lax.dot_general(keys, qc, NT, preferred_element_type=jnp.float32)
-        scores = both[:, :BLOCK]
         d_prob = both[:, BLOCK:]
-        bias = jnp.concatenate(
-            [jnp.full((BLOCK, 1), jnp.where(s <= count, 0.0, -1e30) if 1 <= s <= MAXADJ else 0.0, jnp.float32)
-             for s in range(SLOTS)], axis=0)
-        scores = scores + bias
-        top = jnp.max(scores, axis=0, keepdims=True)
-        expo = jnp.exp(scores - top)
-        prob = expo * (1.0 / jnp.sum(expo, axis=0, keepdims=True))
-        centre = jnp.sum(prob * d_prob, axis=0, keepdims=True)
+        scores = []
+        for s in range(SLOTS):
+            part = both[s * BLOCK:(s + 1) * BLOCK, :BLOCK]
+            scores.append(part + jnp.where(s <= count, 0.0, -1e30) if 1 <= s <= MAXADJ else part)
+        scores = jnp.concatenate(scores, axis=0)
+        expo = jnp.exp(scores - jnp.max(scores, axis=0, keepdims=True))
+        recip = 1.0 / jnp.sum(expo, axis=0, keepdims=True)
+        centre = jnp.sum(expo * d_prob, axis=0, keepdims=True) * recip
+        prob = expo * recip
         d_score = prob * (d_prob - centre)
         mixed = jnp.concatenate([d_score.astype(jnp.bfloat16), prob.astype(jnp.bfloat16)], axis=1)
         rows = jnp.dot(keys_t, mixed, preferred_element_type=jnp.float32)
@@ -227,11 +230,11 @@
 
     def z_copy(d, src, dst, k):
         dest = served(d)
-        return remote(src.at[dest], dst.at[head], z_send.at[k, d], z_recv.at[k, head], (node, dest))
+        return remote(src.at[dest], dst.at[head], z_send.at[k], z_recv.at[k], (node, dest))
 
     def arrive(d):
         source = served(d)
-        remote(packed.at[0], landed.at[source], c_send.at[d], c_recv.at[d], (node, source)).wait_recv()
+        remote(packed.at[0], landed.at[source], c_send, c_recv.at[d], (node, source)).wait_recv()
         pass_copy(d).start()
 
     def direct(k):
@@ -249,25 +252,21 @@
 
         z_copy(2 * k + 1, t1, r1_ref, 0).start()
 
+        @pl.when(jnp.logical_and(carries, k == 1))
+        def _():
+            t, rows, lanes = tile(node)
+            pieces = all_ref.at[pl.ds(0, ways - 1), t, rows, lanes]
+            all_bytes(pieces, a_send, a_recv).wait()
+            loop(1, nodes // CORES, lambda d: plane_copy(node, d).start())
+
     def second(k):
         for d in (2 * k, 2 * k + 1):
             other = landed.at[passed(d)]
-            remote(other, other, f_send.at[d], f_recv.at[d], (node, partner)).wait_recv()
+            remote(other, other, f_send, f_recv.at[d], (node, partner)).wait_recv()
         block(passed(2 * k))
         block(passed(2 * k + 1))
 
     loop(0, reach // 2, direct)
-
-    @pl.when(carries)
-    def _():
-        def landed_piece(d):
-            t, rows, lanes = tile(node)
-            source = lax.rem(me + ways - d, ways)
-            remote(shard.at[t, rows, lanes], all_ref.at[source, t, rows, lanes], a_send.at[d], a_recv.at[d],
-                   around(d)).wait()
-
-        loop(1, ways, landed_piece)
-        loop(1, nodes // CORES, lambda d: plane_copy(node, d).start())
 
     loop(0, reach // 2, second)
 
@@ -320,46 +319,43 @@
 
     def near_copy(d):
         rows, lanes = piece(lax.rem(near_me + d, cross))
-        return remote(gw.at[rows, lanes], near.at[d], n_send.at[d], n_recv.at[d], near_node(d))
+        return remote(gw.at[rows, lanes], near.at[d], n_send, n_recv, near_node(d))
 
     def y_copy(d):
-        return remote(near.at[0], line.at[d], y_send.at[d], y_recv.at[d], y_node(d))
+        return remote(near.at[0], line.at[d], y_send, y_recv, y_node(d))
 
     my_rows, my_lanes = piece(near_me)
 
     def back_copy(d):
-        return remote(line.at[0], out_ref.at[my_rows, my_lanes], g_send.at[d], g_recv.at[d], near_node(d))
+        return remote(line.at[0], out_ref.at[my_rows, my_lanes], g_send, g_recv, near_node(d))
 
     loop(1, cross, lambda d: near_copy(d).start())
 
-    def end_plane(d):
-        source = lax.rem(node + nodes - CORES * d, nodes)
-
-        @pl.when(source // cross < 3)
-        def _():
-            plane_copy(source, d).wait_recv()
-
-    loop(1, nodes // CORES, end_plane)
+    carriers = 3 * xs
+
+    @pl.when(carries)
+    def _():
+        all_bytes(runs.at[pl.ds(0, carriers - 1)], p_send, p_recv).wait_recv()
+
+    @pl.when(jnp.logical_not(carries))
+    def _():
+        all_bytes(runs.at[pl.ds(0, carriers)], p_send, p_recv).wait_recv()
+
     core_copy(core).start()
-    loop(1, cross, lambda d: near_copy(d).wait())
+    all_bytes(near.at[pl.ds(0, cross - 1)], n_send, n_recv).wait()
     total = gw[my_rows, my_lanes]
     for d in range(1, cross):
         total = total + near[d]
     near[0] = total
     loop(1, ys, lambda d: y_copy(d).start())
 
-    def end_first(d):
-        z_copy(d, t1, r1_ref, 0).wait_send()
-        other = lax.rem(head + d, reach)
-        remote(t1.at[0], r1_ref.at[other], z_send.at[0, d], z_recv.at[0, other], around(d)).wait_recv()
-
-    loop(1, reach, end_first)
+    all_bytes(t1.at[pl.ds(0, reach - 1)], z_send.at[0], z_recv.at[0]).wait()
     low_all = low_lanes(BLOCK)
     for p in range(HEADS // 2):
         first = r1_ref[2 * p].astype(jnp.float32)
         second_head = pltpu.roll(r1_ref[2 * p + 1].astype(jnp.float32), 64, 1)
         attn_ref[:, 128 * p:128 * (p + 1)] = jnp.where(low_all, first, second_head).astype(jnp.bfloat16)
-    loop(1, ys, lambda d: y_copy(d).wait())
+    all_bytes(line.at[pl.ds(0, ys - 1)], y_send, y_recv).wait()
     for d in range(1, ys):
         total = total + line[d]
     line[0] = total
@@ -374,30 +370,20 @@
         wq = jnp.concatenate([zeros, all_ref[2 * h, 0], all_ref[2 * h + 1, 0]], axis=0)
         grad = grad + jnp.dot(r1_ref[h], wq, preferred_element_type=jnp.float32)
 
-    def end_last(d):
-        z_copy(d, t2, r2_ref, 1).wait_send()
-        other = lax.rem(head + d, reach)
-        remote(t2.at[0], r2_ref.at[other], z_send.at[1, d], z_recv.at[1, other], around(d)).wait_recv()
-
-    loop(1, reach, end_last)
+    all_bytes(t2.at[pl.ds(0, reach - 1)], z_send.at[1], z_recv.at[1]).wait()
     for h in range(HEADS):
         wvk = jnp.concatenate(
             [all_ref[2 * h, 1], all_ref[2 * h + 1, 1], all_ref[2 * h, 2], all_ref[2 * h + 1, 2]], axis=0)
         grad = grad + jnp.dot(r2_ref[h], wvk, preferred_element_type=jnp.float32)
     gx_ref[...] = grad.astype(jnp.bfloat16)
 
-    def end_back(d):
-        back_copy(d).wait_send()
-        rows, lanes = piece(lax.rem(near_me + cross - d, cross))
-        remote(line.at[0], out_ref.at[rows, lanes], g_send.at[d], g_recv.at[d], near_node(d)).wait_recv()
-
-    loop(1, cross, end_back)
-    loop(1, reach, lambda d: cot_copy(d).wait_send())
-    loop(0, reach, lambda d: pass_copy(d).wait_send())
+    all_bytes(near.at[pl.ds(0, cross - 1)], g_send, g_recv).wait()
+    all_bytes(landed.at[pl.ds(0, reach - 1)], c_send, c_send).wait_send()
+    all_bytes(landed.at[pl.ds(0, reach)], f_send, f_send).wait_send()
 
     @pl.when(carries)
     def _():
-        loop(1, nodes // CORES, lambda d: plane_copy(node, d).wait_send())
+        all_bytes(runs.at[pl.ds(0, nodes // CORES - 1)], p_send, p_recv).wait_send()
 
 
 def finish_kernel(attn_in, gx_in, gw_ref, attn_ref, gx_ref, gq_ref, gk_ref, gv_ref):
@@ -454,10 +440,8 @@
             pltpu.VMEM((HEADS, BLOCK, 128), bf16),
             pltpu.VMEM((HEADS, BLOCK, 128), bf16),
             pltpu.VMEM((ways, 3, cols, width), bf16),
-            dma((9,)), dma, dma, dma((ways // 2,)), dma((ways // 2,)), dma((ways // 2,)), dma((ways // 2,)), dma((ways,)), dma((ways,)),
-            dma((nodes // CORES,)), dma((nodes // CORES,)), dma, dma,
-            dma((2, ways // 2)), dma((2, ways // 2)), dma((cross,)), dma((cross,)),
-            dma((ys,)), dma((ys,)), dma((cross,)), dma((cross,)),
+            dma((9,)), dma, dma, dma, dma((ways // 2,)), dma, dma((ways // 2,)), dma, dma, dma, dma, dma, dma,
+            dma((2,)), dma((2,)), dma, dma, dma, dma, dma, dma,
         ],
         compiler_params=params(collective_id=0, has_side_effects=True),
         cost_estimate=pl.CostEstimate(flops=16 * 2 * 1024 * 256 * 384, bytes_accessed=8 << 20, transcendentals=1 << 21),

time: 60.5 us -> 57.3 us (0.947)
  Pallas kernels: 59.7 us -> 56.5 us
    pallas_call x1, Pallas kernels: 57.9 us -> 54.7 us  [local(): pl.pallas_call(functools.partial(layer_kernel, ways, xs, ys), out_shape=(...]
where the time goes in v3:
time: 57.3 us; the launch traced here: 57.1 us
  Pallas kernels  56.5 us (99%)
  between operations  0.64 us (1%)
    pallas_call x1, Pallas kernels, local(): pl.pallas_call(functools.partial(layer_kernel, ways, xs, ys), out_shape=(...  54.7 us
    pallas_call x1, Pallas kernels, local(): pl.pallas_call(finish_kernel, out_shape=(sds((BLOCK, width), bf16), sds((...  1.82 us

profile of v3, /device:TPU:1, one launch (start us, length us, event | category | flops | bytes accessed | tf_op | source)
XLA Modules:
  0.0 57.1 jit_solution(15395952695589354530)
XLA Ops:
  0.6 54.7 %shard_map.119 = (bf16[128,512]{1,0:T(8,128)(2,1)}, bf16[128,512]{1,0:T(8,128)(2,1)}, f32[96,512]{1,0:T(8,128)}) custom-call(s32[4,16]{1,0:T(4,128)} %bitcast.13, s32[3,1,16]{2,1,0:T(1,128)} %perms_hbm.1, s32[16]{0:T(128)} %counts_hbm.1, bf16[32,512]{1,0:T(8,128)(2,1)} %bitcast.10, bf16[32,512]{1,0:T(8,128)(2,1)} %bitcast.11, bf16[32,512]{1,0:T(8,128)(2,1)} %bitcast.12, ...), custom_call_target="tpu_custom_call" | custom-call | flops 3221225472 | bytes 8388608 | tf_op jit(solution)/shard_map/pallas_call | solution.py:412
  55.3 1.8 %shard_map.120 = (bf16[128,512]{1,0:T(8,128)(2,1)}, bf16[128,512]{1,0:T(8,128)(2,1)}, f32[32,512]{1,0:T(8,128)}, f32[32,512]{1,0:T(8,128)}, f32[32,512]{1,0:T(8,128)}) custom-call(bf16[128,512]{1,0:T(8,128)(2,1)} %get-tuple-element.13.attn_in, bf16[128,512]{1,0:T(8,128)(2,1)} %get-tuple-element.14.gx_in, f32[96,512]{1,0:T(8,128)} %get-tuple-element.15.gw_ref), custom_call_target="tpu_custom_call" | custom-call | bytes 1048576 | tf_op jit(solution)/shard_map/pallas_call | solution.py:449

commit v4 on v3

--- a/solution.py
+++ b/solution.py
@@ -200,11 +200,11 @@
             kv[b] = part[:, 128:].astype(jnp.bfloat16)
             kvt[b] = jnp.transpose(part[:, 128:]).astype(jnp.bfloat16)
 
-    def block(b):
+    def block(b, serve):
         ids = [plan[0, s * ways + b] for s in range(SLOTS)]
         count = counts[b]
         keys = jnp.concatenate([kv[i] for i in ids], axis=0)
-        keys_t = jnp.concatenate([kvt[i] for i in ids], axis=1)
+        keys_t = jnp.concatenate([kvt[i] if serve else kvt[i, HD:, :] for i in ids], axis=1)
         got = landed[b].astype(jnp.float32)
         cot_rows = jnp.concatenate(
             [jnp.where(low, got, 0.0), jnp.where(low, pltpu.roll(got, 64, 1), 0.0)], axis=0).astype(jnp.bfloat16)
@@ -222,9 +222,13 @@
         prob = expo * recip
         d_score = prob * (d_prob - centre)
         mixed = jnp.concatenate([d_score.astype(jnp.bfloat16), prob.astype(jnp.bfloat16)], axis=1)
-        rows = jnp.dot(keys_t, mixed, preferred_element_type=jnp.float32)
-        d_query = rows[HD:, :BLOCK] * 0.125
-        both_t = jnp.concatenate([rows[:HD, BLOCK:], d_query], axis=0)
+        if serve:
+            rows = jnp.dot(keys_t, mixed, preferred_element_type=jnp.float32)
+            values, d_query = rows[:HD, BLOCK:], rows[HD:, :BLOCK]
+        else:
+            d_query = jnp.dot(keys_t, mixed[:, :BLOCK], preferred_element_type=jnp.float32)
+            values = jnp.zeros_like(d_query)
+        both_t = jnp.concatenate([values, d_query * 0.125], axis=0)
         t1[b] = jnp.transpose(both_t).astype(jnp.bfloat16)
         terms[b] = jnp.dot(mixed, qc, preferred_element_type=jnp.float32).reshape(SLOTS, BLOCK, 128)
 
@@ -243,8 +247,8 @@
             arrive(2 * k)
 
         arrive(2 * k + 1)
-        block(served(2 * k))
-        block(served(2 * k + 1))
+        block(served(2 * k), True)
+        block(served(2 * k + 1), True)
 
         @pl.when(k > 0)
         def _():
@@ -263,8 +267,8 @@
         for d in (2 * k, 2 * k + 1):
             other = landed.at[passed(d)]
             remote(other, other, f_send, f_recv.at[d], (node, partner)).wait_recv()
-        block(passed(2 * k))
-        block(passed(2 * k + 1))
+        block(passed(2 * k), False)
+        block(passed(2 * k + 1), False)
 
     loop(0, reach // 2, direct)
 

time: 57.3 us -> 59.5 us (1.038)
  Pallas kernels: 56.5 us -> 58.6 us
    pallas_call x1, Pallas kernels: 54.7 us -> 56.8 us  [local(): pl.pallas_call(functools.partial(layer_kernel, ways, xs, ys), out_shape=(...]
where the time goes in v4:
time: 59.5 us; the launch traced here: 59.3 us
  Pallas kernels  58.6 us (98%)
  between operations  0.64 us (1%)
    pallas_call x1, Pallas kernels, local(): pl.pallas_call(functools.partial(layer_kernel, ways, xs, ys), out_shape=(...  56.8 us
    pallas_call x1, Pallas kernels, local(): pl.pallas_call(finish_kernel, out_shape=(sds((BLOCK, width), bf16), sds((...  1.82 us

profile of v4, /device:TPU:1, one launch (start us, length us, event | category | flops | bytes accessed | tf_op | source)
XLA Modules:
  0.0 59.3 jit_solution(17256845552917640619)
XLA Ops:
  0.6 56.8 %shard_map.119 = (bf16[128,512]{1,0:T(8,128)(2,1)}, bf16[128,512]{1,0:T(8,128)(2,1)}, f32[96,512]{1,0:T(8,128)}) custom-call(s32[4,16]{1,0:T(4,128)} %bitcast.13, s32[3,1,16]{2,1,0:T(1,128)} %perms_hbm.1, s32[16]{0:T(128)} %counts_hbm.1, bf16[32,512]{1,0:T(8,128)(2,1)} %bitcast.10, bf16[32,512]{1,0:T(8,128)(2,1)} %bitcast.11, bf16[32,512]{1,0:T(8,128)(2,1)} %bitcast.12, ...), custom_call_target="tpu_custom_call" | custom-call | flops 3221225472 | bytes 8388608 | tf_op jit(solution)/shard_map/pallas_call | solution.py:416
  57.5 1.8 %shard_map.120 = (bf16[128,512]{1,0:T(8,128)(2,1)}, bf16[128,512]{1,0:T(8,128)(2,1)}, f32[32,512]{1,0:T(8,128)}, f32[32,512]{1,0:T(8,128)}, f32[32,512]{1,0:T(8,128)}) custom-call(bf16[128,512]{1,0:T(8,128)(2,1)} %get-tuple-element.13.attn_in, bf16[128,512]{1,0:T(8,128)(2,1)} %get-tuple-element.14.gx_in, f32[96,512]{1,0:T(8,128)} %get-tuple-element.15.gw_ref), custom_call_target="tpu_custom_call" | custom-call | bytes 1048576 | tf_op jit(solution)/shard_map/pallas_call | solution.py:453
